TPU v7x, 32 devices: a whole 2x2x4 slice. The times are simulated.
32 devices in a mesh: col: 4 (over x, core), af: 8 (over z, y).
Axes of the slice: x: 2, y: 2, z: 4, core: 2. Of those that a mesh axis runs over, the one named last changes fastest.
Arguments:
- coarse_state: float32 [3, 8, 128, 1024], P(None, None, 'af', 'col'), may hold values from 0.1 to 2
- coarse_kappa: float32 [8, 128, 1024], P(None, 'af', 'col'), may hold values from 0.25 to 1
- coarse_rate: float32 [8, 128, 1024], P(None, 'af', 'col'), may hold values from 0.5 to 6
- fine_state: float32 [128, 3, 32, 1024], P(('col', 'af')), may hold values from 0.1 to 2
- fine_kappa: float32 [128, 32, 1024], P(('col', 'af')), may hold values from 0.25 to 1
- fine_rate: float32 [128, 32, 1024], P(('col', 'af')), may hold values from 0.5 to 6
- boxes: int32 [128, 2], replicated, may hold values from 0 to 127, as said below
- cover: int32 [16, 128], replicated, may hold values from -1 to 127, as said below
Outputs:
- coarse_out: float32 [3, 8, 128, 1024], P(None, None, 'af', 'col')
- fine_out: float32 [128, 3, 32, 1024], P(('col', 'af'))
Inputs may be any that keep to these rules, and one draw needn't show every extreme that they name: `boxes`: A patch's block spans all 8 planes; it lies in the 32 block rows of one col index, never in the first or last of them nor in the slab's first or last block column, and no two patches share a face. The patches whose blocks lie in one col index's rows are the rows of the fine arrays held by that col index, in no particular order. The 2 block columns of one af index hold at most 10 patches, and in every col index some af index holds exactly that many. cover[bx, by] is the patch whose block is (bx, by), or -1 where none is; it agrees with boxes, and every patch appears once.
All inputs are finite; a program needn't handle non-finite values.
Results may differ from a plain program's by a relative error of at most 0.0003.
Values sent between devices are 32-bit elements; how exact they have to be, the bound alone decides.
No kernel may reach another device: no remote copies, remote signals or barrier semaphores. Data moves between devices by JAX's collectives and lax.ppermute only.
A program may use at most 192 MiB of HBM per device.

v0:
```python
import jax
import jax.numpy as jnp
from jax import lax
from jax.sharding import PartitionSpec as P

NZC = 8
RATIO = 4
BLK = 8


DT_COARSE = 1.0 / 28.0
DIFFUSE = (1.0, 0.7, 0.45)
NEIGHBOURS = ((1, 0, 0), (-1, 0, 0), (0, 1, 0), (0, -1, 0), (0, 0, 1), (0, 0, -1))


def with_halo(cells, sides, width):
    for axis, dim in sides:
        count = lax.axis_size(axis)
        ends = count - 1
        head = lax.slice_in_dim(cells, 0, width, axis=dim)
        tail = lax.slice_in_dim(cells, cells.shape[dim] - width, cells.shape[dim], axis=dim)
        cells = jnp.concatenate(
            [
                lax.ppermute(tail, axis, [(i, (i + 1) % count) for i in range(ends)]),
                cells,
                lax.ppermute(head, axis, [((i + 1) % count, i) for i in range(ends)]),
            ],
            axis=dim,
        )
    return cells


def harmonic(first, second):
    summed = first + second
    positive = summed > 0.0
    return jnp.where(positive, 2.0 * first * second / jnp.where(positive, summed, 1.0), 0.0)


def combine(center, conduct, neighbour_list, reaction, inv_square, step_size):
    summed = jnp.zeros_like(center)
    for values, coeffs in neighbour_list:
        summed = summed + harmonic(conduct, coeffs) * (values - center)
    spread = (
        jnp.stack([DIFFUSE[0] * summed[0], DIFFUSE[1] * summed[1], DIFFUSE[2] * summed[2]])
        * inv_square
    )
    forward = reaction * (center[0] * center[1] - center[2])
    change = spread + jnp.stack([-forward, -forward, forward])
    return center + step_size * change


def window(values, step_z, step_x, step_y):
    depth_len = values.shape[-3] - 2
    across = values.shape[-2] - 2
    along_len = values.shape[-1] - 2
    return values[
        ...,
        1 + step_z : 1 + step_z + depth_len,
        1 + step_x : 1 + step_x + across,
        1 + step_y : 1 + step_y + along_len,
    ]


def coarse_advance(padded_xy, conduct_xy, reaction):
    padded = jnp.pad(padded_xy, ((0, 0), (1, 1), (0, 0), (0, 0)))
    conduct = jnp.pad(conduct_xy, ((1, 1), (0, 0), (0, 0)))
    neighbour_list = [
        (
            window(padded, offsets[0], offsets[1], offsets[2]),
            window(conduct, offsets[0], offsets[1], offsets[2]),
        )
        for offsets in NEIGHBOURS
    ]
    return combine(
        window(padded, 0, 0, 0), window(conduct, 0, 0, 0), neighbour_list, reaction, 1.0, DT_COARSE
    )


def upsample(strips):
    return jnp.repeat(jnp.repeat(strips, RATIO, axis=-2), RATIO, axis=-1)


def patch_step(fields, conduct, reaction, strips):
    ghosts = upsample(strips)
    edge_len = ghosts.shape[-1]
    position = lax.broadcasted_iota(jnp.int32, (1, edge_len * edge_len), 1)
    column = position % edge_len
    row_pos = position // edge_len
    zero_fields = jnp.zeros_like(fields[:, :1])
    zero_conduct = jnp.zeros_like(conduct[:1])
    upward = (
        jnp.concatenate([fields[:, 1:], zero_fields], axis=1),
        jnp.concatenate([conduct[1:], zero_conduct], axis=0),
    )
    downward = (
        jnp.concatenate([zero_fields, fields[:, :-1]], axis=1),
        jnp.concatenate([zero_conduct, conduct[:-1]], axis=0),
    )
    last_row = row_pos == edge_len - 1
    first_row = row_pos == 0
    last_col = column == edge_len - 1
    first_col = column == 0
    next_x = (
        jnp.where(
            last_row, jnp.tile(ghosts[1], (1, 1, edge_len)), jnp.roll(fields, -edge_len, axis=-1)
        ),
        jnp.where(last_row, conduct, jnp.roll(conduct, -edge_len, axis=-1)),
    )
    prev_x = (
        jnp.where(
            first_row, jnp.tile(ghosts[0], (1, 1, edge_len)), jnp.roll(fields, edge_len, axis=-1)
        ),
        jnp.where(first_row, conduct, jnp.roll(conduct, edge_len, axis=-1)),
    )
    next_y = (
        jnp.where(
            last_col, jnp.repeat(ghosts[3], edge_len, axis=-1), jnp.roll(fields, -1, axis=-1)
        ),
        jnp.where(last_col, conduct, jnp.roll(conduct, -1, axis=-1)),
    )
    prev_y = (
        jnp.where(
            first_col, jnp.repeat(ghosts[2], edge_len, axis=-1), jnp.roll(fields, 1, axis=-1)
        ),
        jnp.where(first_col, conduct, jnp.roll(conduct, 1, axis=-1)),
    )
    return combine(
        fields,
        conduct,
        [upward, downward, next_x, prev_x, next_y, prev_y],
        reaction,
        float(RATIO * RATIO),
        DT_COARSE / RATIO,
    )


def restrict(fields):
    shaped = fields.reshape(3, NZC, RATIO, BLK, RATIO, BLK, RATIO)
    return jnp.mean(shaped, axis=(2, 4, 6)).reshape(-1)


def rim_rows(outer, block_cols, block_rows):
    species, planes, reach_x, cells_y = outer.shape
    padded_y = jnp.pad(outer, ((0, 0), (0, 0), (0, 0), (1, 1)))
    collected = []
    for column in range(block_cols):
        base_x = BLK * column
        lower_x = (
            outer[:, :, base_x, :].reshape(species, planes, block_rows, BLK).transpose(2, 0, 1, 3)
        )
        upper_x = (
            outer[:, :, base_x + BLK + 1, :]
            .reshape(species, planes, block_rows, BLK)
            .transpose(2, 0, 1, 3)
        )
        lower_y = padded_y[:, :, base_x + 1 : base_x + 1 + BLK, 0:cells_y:BLK].transpose(3, 0, 1, 2)
        upper_y = padded_y[
            :, :, base_x + 1 : base_x + 1 + BLK, BLK + 1 : cells_y + 2 : BLK
        ].transpose(3, 0, 1, 2)
        face_rows = jnp.stack([lower_x, upper_x, lower_y, upper_y], axis=1)
        collected.append(face_rows.reshape(block_rows, -1))
    return jnp.concatenate(collected, axis=0)


def sum_sources(received):
    return jnp.sum(received, axis=0)


def per_device(
    coarse_state, coarse_kappa, coarse_rate, fine_state, fine_kappa, fine_rate, boxes, cover
):
    af_count = lax.axis_size("af")
    af_index = lax.axis_index("af")
    col_index = lax.axis_index("col")
    slot_count = fine_state.shape[0]
    cells_x = coarse_state.shape[2]
    cells_y = coarse_state.shape[3]
    block_cols = cells_x // BLK
    block_rows = cells_y // BLK
    group_size = af_count * slot_count
    group_base = col_index * group_size
    stacked = jnp.concatenate([coarse_state, coarse_kappa[None]], axis=0)
    widened = with_halo(stacked, (("col", 3), ("af", 2)), 1)
    coarse_new = coarse_advance(widened[:3], widened[3], coarse_rate)
    outer_new = with_halo(coarse_new, (("af", 2),), 1)
    outer_old = widened[:3, :, :, 1:-1]
    group_boxes = lax.dynamic_slice_in_dim(boxes, group_base, group_size, 0)
    local_x = group_boxes[:, 0] - af_index * block_cols
    local_y = group_boxes[:, 1] - col_index * block_rows
    inside = (local_x >= 0) & (local_x < block_cols) & (local_y >= 0) & (local_y < block_rows)
    block_ids = jnp.where(inside, local_x * block_rows + local_y, -1)
    targets = (
        block_ids[:, None] == jnp.arange(block_cols * block_rows, dtype=jnp.int32)[None, :]
    ).astype(jnp.float32)
    earlier = rim_rows(outer_old, block_cols, block_rows)
    updated = rim_rows(outer_new, block_cols, block_rows)
    fields = fine_state
    for substep in range(RATIO):
        fraction = substep / RATIO
        current = earlier + fraction * (updated - earlier)
        send_rows = jnp.dot(targets, current, precision=lax.Precision.HIGHEST)
        strips = sum_sources(
            lax.all_to_all(
                send_rows.reshape(af_count, slot_count, current.shape[1]),
                "af",
                split_axis=0,
                concat_axis=0,
                tiled=True,
            )
        )
        strips = strips.reshape(slot_count, 4, 3, NZC, BLK)
        fields = jax.vmap(patch_step)(fields, fine_kappa, fine_rate, strips)
    averages = jax.vmap(restrict)(fields)
    cover_mine = lax.dynamic_slice(
        cover, (af_index * block_cols, col_index * block_rows), (block_cols, block_rows)
    ).reshape(-1)
    wanted = cover_mine - group_base
    portion = lax.all_gather(averages, "af", axis=0, tiled=True)
    selector = (wanted[:, None] == jnp.arange(portion.shape[0], dtype=jnp.int32)[None, :]).astype(
        jnp.float32
    )
    placed = jnp.dot(selector, portion, precision=lax.Precision.HIGHEST)
    placed = (
        placed.reshape(block_cols, block_rows, 3, NZC, BLK, BLK)
        .transpose(2, 3, 0, 4, 1, 5)
        .reshape(3, NZC, cells_x, cells_y)
    )
    covered = (cover_mine >= 0).reshape(block_cols, block_rows)
    covered = jnp.repeat(jnp.repeat(covered, BLK, axis=0), BLK, axis=1)
    coarse_out = jnp.where(covered[None, None], placed, coarse_new)
    return (coarse_out, fields)


def solution(mesh):
    return jax.shard_map(
        per_device,
        mesh=mesh,
        in_specs=(
            P(None, None, "af", "col"),
            P(None, "af", "col"),
            P(None, "af", "col"),
            P(("col", "af"), None, None, None),
            P(("col", "af"), None, None),
            P(("col", "af"), None, None),
            P(),
            P(),
        ),
        out_specs=(P(None, None, "af", "col"), P(("col", "af"), None, None, None)),
        check_vma=False,
    )
```

profile of v0, /device:TPU:2, one launch (start us, length us, event | category | flops | bytes accessed | tf_op | source)
XLA Modules:
  0.0 532.2 jit_solution(10903677101799349000)
XLA Ops:
  75.7 4.9 collective-permute-start.4
  122.8 5.4 %all-to-all-start = ((f32[8,4,768]{2,1,0:T(4,128)}), f32[8,4,768]{2,1,0:T(4,128)S(1)}, u32[]{:S(2)}, u32[]{:S(2)}) async-start(f32[8,4,768]{2,1,0:T(4,128)} %reshape.321), calls=%async_computation | async-start | bytes 196608 | tf_op jit(solution)/shard_map/all_to_all | solution.py:203
  135.3 5.7 %all-to-all-start.1 = ((f32[8,4,768]{2,1,0:T(4,128)}), f32[8,4,768]{2,1,0:T(4,128)}, u32[]{:S(2)}, u32[]{:S(2)}) async-start(f32[8,4,768]{2,1,0:T(4,128)} %reshape.327), calls=%async_computation.1 | async-start | bytes 196608 | tf_op jit(solution)/shard_map/all_to_all | solution.py:203
  150.6 5.9 %reshape.325 = f32[4,3,32,1024]{3,2,0,1:T(8,128)} reshape(f32[4,3,32,32,32]{4,3,2,0,1:T(8,128)} %broadcast_in_dim.329) | data formatting | bytes 3145728 | tf_op jit(solution)/shard_map/vmap()/reshape | solution.py:117
  160.4 5.9 %reshape.326 = f32[4,3,32,1024]{3,2,0,1:T(8,128)} reshape(f32[4,3,32,32,32]{4,3,2,0,1:T(8,128)} %broadcast_in_dim.332) | data formatting | bytes 3145728 | tf_op jit(solution)/shard_map/vmap()/reshape | solution.py:123
  169.4 5.9 %tile.82 = f32[4,3,32,1024]{3,2,0,1:T(8,128)} reshape(f32[4,3,32,32,32]{4,3,2,0,1:T(8,128)} %tile.81) | data formatting | bytes 3145728 | tf_op jit(solution)/shard_map/vmap()/tile | solution.py:105
  178.4 6.0 %tile.85 = f32[4,3,32,1024]{3,2,0,1:T(8,128)} reshape(f32[4,3,32,32,32]{4,3,2,0,1:T(8,128)} %tile.84) | data formatting | bytes 3145728 | tf_op jit(solution)/shard_map/vmap()/tile | solution.py:111
  184.4 7.7 %fusion.5 = f32[4,3,32,1024]{3,2,0,1:T(8,128)S(1)} fusion(f32[4,3,32,1024]{3,2,0,1:T(8,128)} %tile.82, f32[4,3,32,32]{3,2,0,1:T(8,128)} %get-tuple-element.69, f32[4,3,32,992]{3,2,0,1:T(8,128)} %get-tuple-element.71, f32[4,3,32,1024]{3,2,0,1:T(8,128)} %tile.85, f32[4,3,32,992]{3,2,0,1:T(8,128)} %get-tuple-element.70, f32[4,3,32,32]{3,2,0,1:T(8,128)} %get-tuple-element.68, ...), kind=kLoop, calls=%fused_computation.8 | loop fusion | flops 9830400 | bytes 21925888 | tf_op jit(solution)/shard_map/vmap()/add | solution.py:42
  201.9 6.2 %all-to-all-start.2 = ((f32[8,4,768]{2,1,0:T(4,128)}), f32[8,4,768]{2,1,0:T(4,128)}, u32[]{:S(2)}, u32[]{:S(2)}) async-start(f32[8,4,768]{2,1,0:T(4,128)} %reshape.333), calls=%async_computation.2 | async-start | bytes 196608 | tf_op jit(solution)/shard_map/all_to_all | solution.py:203
  217.7 4.8 broadcast_in_dim.335
  222.5 5.9 %reshape.331 = f32[4,3,32,1024]{3,2,0,1:T(8,128)} reshape(f32[4,3,32,32,32]{4,3,2,0,1:T(8,128)} %broadcast_in_dim.335) | data formatting | bytes 3145728 | tf_op jit(solution)/shard_map/vmap()/reshape | solution.py:117
  230.1 4.8 broadcast_in_dim.336
  235.0 5.9 %reshape.332 = f32[4,3,32,1024]{3,2,0,1:T(8,128)} reshape(f32[4,3,32,32,32]{4,3,2,0,1:T(8,128)} %broadcast_in_dim.336) | data formatting | bytes 3145728 | tf_op jit(solution)/shard_map/vmap()/reshape | solution.py:123
  246.5 5.9 %tile.88 = f32[4,3,32,1024]{3,2,0,1:T(8,128)} reshape(f32[4,3,32,32,32]{4,3,2,0,1:T(8,128)} %tile.87) | data formatting | bytes 3145728 | tf_op jit(solution)/shard_map/vmap()/tile | solution.py:105
  258.0 5.9 %tile.91 = f32[4,3,32,1024]{3,2,0,1:T(8,128)} reshape(f32[4,3,32,32,32]{4,3,2,0,1:T(8,128)} %tile.90) | data formatting | bytes 3145728 | tf_op jit(solution)/shard_map/vmap()/tile | solution.py:111
  264.0 8.3 %fusion.21 = f32[4,3,32,1024]{3,2,0,1:T(8,128)S(1)} fusion(f32[4,3,32,1024]{3,2,0,1:T(8,128)} %tile.88, f32[4,3,32,32]{3,2,0,1:T(8,128)} %get-tuple-element.56, f32[4,3,32,992]{3,2,0,1:T(8,128)} %get-tuple-element.58, f32[4,3,32,1024]{3,2,0,1:T(8,128)} %tile.91, f32[4,3,32,992]{3,2,0,1:T(8,128)} %get-tuple-element.57, ...), kind=kLoop, calls=%fused_computation.29 | loop fusion | flops 12976128 | bytes 24547328 | tf_op jit(solution)/shard_map/vmap()/add | solution.py:42
  283.9 6.3 %all-to-all-start.3 = ((f32[8,4,768]{2,1,0:T(4,128)}), f32[8,4,768]{2,1,0:T(4,128)}, u32[]{:S(2)}, u32[]{:S(2)}) async-start(f32[8,4,768]{2,1,0:T(4,128)} %reshape.339), calls=%async_computation.3 | async-start | bytes 196608 | tf_op jit(solution)/shard_map/all_to_all | solution.py:203
  299.7 4.8 broadcast_in_dim.339
  304.6 5.9 %reshape.337 = f32[4,3,32,1024]{3,2,0,1:T(8,128)} reshape(f32[4,3,32,32,32]{4,3,2,0,1:T(8,128)} %broadcast_in_dim.339) | data formatting | bytes 3145728 | tf_op jit(solution)/shard_map/vmap()/reshape | solution.py:117
  317.0 5.9 %reshape.338 = f32[4,3,32,1024]{3,2,0,1:T(8,128)} reshape(f32[4,3,32,32,32]{4,3,2,0,1:T(8,128)} %broadcast_in_dim.340) | data formatting | bytes 3145728 | tf_op jit(solution)/shard_map/vmap()/reshape | solution.py:123
  328.5 5.9 %tile.94 = f32[4,3,32,1024]{3,2,0,1:T(8,128)} reshape(f32[4,3,32,32,32]{4,3,2,0,1:T(8,128)} %tile.93) | data formatting | bytes 3145728 | tf_op jit(solution)/shard_map/vmap()/tile | solution.py:105
  340.1 5.9 %tile.97 = f32[4,3,32,1024]{3,2,0,1:T(8,128)} reshape(f32[4,3,32,32,32]{4,3,2,0,1:T(8,128)} %tile.96) | data formatting | bytes 3145728 | tf_op jit(solution)/shard_map/vmap()/tile | solution.py:111
  346.1 10.1 %fusion.37 = f32[4,3,32,1024]{3,2,0,1:T(8,128)S(1)} fusion(f32[4,3,32,1024]{3,2,0,1:T(8,128)} %tile.94, f32[4,3,32,32]{3,2,0,1:T(8,128)} %get-tuple-element.43, f32[4,3,32,992]{3,2,0,1:T(8,128)} %get-tuple-element.45, f32[4,3,32,1024]{3,2,0,1:T(8,128)} %tile.97, f32[4,3,32,992]{3,2,0,1:T(8,128)} %get-tuple-element.44, ...), kind=kLoop, calls=%fused_computation.50 | loop fusion | flops 16121856 | bytes 27168768 | tf_op jit(solution)/shard_map/vmap()/add | solution.py:42
  374.1 5.9 %reshape.343 = f32[4,3,32,1024]{3,2,0,1:T(8,128)} reshape(f32[4,3,32,32,32]{4,3,2,0,1:T(8,128)} %broadcast_in_dim.343) | data formatting | bytes 3145728 | tf_op jit(solution)/shard_map/vmap()/reshape | solution.py:117
  383.9 5.9 %reshape.344 = f32[4,3,32,1024]{3,2,0,1:T(8,128)} reshape(f32[4,3,32,32,32]{4,3,2,0,1:T(8,128)} %broadcast_in_dim.344) | data formatting | bytes 3145728 | tf_op jit(solution)/shard_map/vmap()/reshape | solution.py:123
  392.8 5.9 %tile.100 = f32[4,3,32,1024]{3,2,0,1:T(8,128)} reshape(f32[4,3,32,32,32]{4,3,2,0,1:T(8,128)} %tile.99) | data formatting | bytes 3145728 | tf_op jit(solution)/shard_map/vmap()/tile | solution.py:105
  401.9 6.1 %tile.103 = f32[4,3,32,1024]{3,2,0,1:T(8,128)} reshape(f32[4,3,32,32,32]{4,3,2,0,1:T(8,128)} %tile.102) | data formatting | bytes 3145728 | tf_op jit(solution)/shard_map/vmap()/tile | solution.py:111
  407.9 7.3 %fusion.50 = f32[4,3,32,1024]{3,2,0,1:T(8,128)S(1)} fusion(f32[4,3,32,1024]{3,2,0,1:T(8,128)} %tile.100, f32[4,3,32,1024]{3,2,0,1:T(8,128)} %tile.103, f32[4,3,32,1024]{3,2,0,1:T(8,128)} %reshape.343, f32[4,3,32,1024]{3,2,0,1:T(8,128)} %reshape.344, f32[4,32,1024]{2,1,0:T(8,128)} %get-tuple-element.95, f32[4,32,1024]{2,1,0:T(8,128)S(1)} %copy-done.21, ...), kind=kLoop, calls=%fused_computation.68 | loop fusion | flops 9830400 | bytes 21925888 | tf_op jit(solution)/shard_map/vmap()/add | solution.py:42
  416.9 53.4 %reshape.345 = f32[4,3,8,4,8,4,8,4]{7,6,5,4,3,2,1,0:T(8,128)} reshape(f32[4,3,32,1024]{3,2,1,0:T(8,128)S(1)} %bitcast_add_fusion) | data formatting | bytes 3145728 | tf_op jit(solution)/shard_map/vmap()/reshape | solution.py:138
  470.3 17.8 %reduce_sum.49 = f32[4,3,8,8,8]{4,3,2,1,0:T(8,128)S(1)} reduce(f32[4,3,8,4,8,4,8,4]{7,6,5,4,3,2,1,0:T(8,128)} %reshape.345, f32[]{:T(128)} %constant.92.clone.1), dimensions={3,5,7}, to_apply=%region_4.5 | reduce | flops 387072 | bytes 1597444 | tf_op jit(solution)/shard_map/vmap()/reduce_sum | solution.py:139
  488.3 31.2 %all-gather = f32[8,4,1536]{2,1,0:T(4,128)S(1)} all-gather(f32[1,4,1536]{2,1,0:T(4,128)S(1)} %reshape.348), channel_id=1, replica_groups=mesh['col'=4,'af'=8] {'af'}, dimensions={0}, use_global_device_ids=true | all-gather | bytes 221184 | tf_op jit(solution)/shard_map/all_gather | solution.py:218
  525.3 5.7 %reshape.347 = f32[3,8,16,256]{3,2,1,0:T(8,128)S(1)} reshape(f32[3,8,2,8,32,8]{5,4,3,2,1,0:T(8,128)} %copy.314) | data formatting | bytes 786432 | tf_op jit(solution)/shard_map/reshape | solution.py:226
  (367 shorter events, 250.9 us)
Async XLA Ops:
  0.6 23.8 %copy-start = (s32[128,2]{0,1:T(2,128)S(1)}, s32[128,2]{0,1:T(2,128)}, u32[]{:S(2)}) copy-start(s32[128,2]{0,1:T(2,128)} %param.14) | copy-start | bytes 3076
  2.6 39.9 %collective-permute-start = (f32[4,8,16,1]{3,2,1,0:T(8,128)}, f32[4,8,16,1]{3,2,1,0:T(8,128)}, u32[]{:S(2)}, u32[]{:S(2)}) collective-permute-start(f32[4,8,16,1]{3,2,1,0:T(8,128)} %get-tuple-element.108), channel_id=1, source_target_pairs={{0,8},{8,16},{16,24},{1,9},{9,17},{17,25},{2,10},{10,18},{18,26},{... | collective-permute-start | bytes 6152 | tf_op jit(solution)/shard_map/ppermute | solution.py:24
  4.6 38.0 %collective-permute-start.1 = (f32[4,8,16,1]{3,2,1,0:T(8,128)}, f32[4,8,16,1]{3,2,1,0:T(8,128)}, u32[]{:S(2)}, u32[]{:S(2)}) collective-permute-start(f32[4,8,16,1]{3,2,1,0:T(8,128)} %get-tuple-element.109), channel_id=1, source_target_pairs={{8,0},{16,8},{24,16},{9,1},{17,9},{25,17},{10,2},{18,10},{26,18},{... | collective-permute-start | bytes 6152 | tf_op jit(solution)/shard_map/ppermute | solution.py:26
  10.0 174.4 %copy-start.70 = (pred[1024]{0:T(1024)(128)(4,1)}, pred[1024]{0:T(1024)(128)(4,1)S(1)}, u32[]{:S(2)}) copy-start(pred[1024]{0:T(1024)(128)(4,1)S(1)} %get-tuple-element.121) | copy-start | bytes 3076
  10.0 174.4 %copy-start.73 = (pred[1024]{0:T(1024)(128)(4,1)}, pred[1024]{0:T(1024)(128)(4,1)S(1)}, u32[]{:S(2)}) copy-start(pred[1024]{0:T(1024)(128)(4,1)S(1)} %get-tuple-element.122) | copy-start | bytes 3076
  10.6 173.8 %copy-start.76 = (pred[1024]{0:T(1024)(128)(4,1)}, pred[1024]{0:T(1024)(128)(4,1)S(1)}, u32[]{:S(2)}) copy-start(pred[1024]{0:T(1024)(128)(4,1)S(1)} %get-tuple-element.123) | copy-start | bytes 3076
  26.3 319.7 %copy-start.6 = (f32[1,4,32,1024]{3,2,1,0:T(8,128)}, f32[1,4,32,1024]{3,2,1,0:T(8,128)S(1)}, u32[]{:S(2)}) copy-start(f32[1,4,32,1024]{3,2,1,0:T(8,128)S(1)} %get-tuple-element.16) | copy-start | bytes 1572868
  26.3 319.7 %copy-start.8 = (f32[4,32,1024]{2,1,0:T(8,128)}, f32[4,32,1024]{2,1,0:T(8,128)S(1)}, u32[]{:S(2)}) copy-start(f32[4,32,1024]{2,1,0:T(8,128)S(1)} %get-tuple-element.17) | copy-start | bytes 1572868
  45.0 7.0 %collective-permute-start.2 = (f32[4,8,1,258]{3,1,2,0:T(8,128)S(1)}, f32[4,8,1,258]{3,1,2,0:T(8,128)S(1)}, u32[]{:S(2)}, u32[]{:S(2)}) collective-permute-start(f32[4,8,1,258]{3,1,2,0:T(8,128)S(1)} %get-tuple-element.89), channel_id=1, source_target_pairs={{0,1},{1,2},{2,3},{3,4},{4,5},{5,6},{6,7},{8,9},{9,10},{10,11},{11... | collective-permute-start | bytes 99080 | tf_op jit(solution)/shard_map/ppermute | solution.py:24
  48.5 6.0 %collective-permute-start.3 = (f32[4,8,1,258]{3,1,2,0:T(8,128)S(1)}, f32[4,8,1,258]{3,1,2,0:T(8,128)S(1)}, u32[]{:S(2)}, u32[]{:S(2)}) collective-permute-start(f32[4,8,1,258]{3,1,2,0:T(8,128)S(1)} %get-tuple-element.88), channel_id=1, source_target_pairs={{1,0},{2,1},{3,2},{4,3},{5,4},{6,5},{7,6},{9,8},{10,9},{11,10},{12... | collective-permute-start | bytes 99080 | tf_op jit(solution)/shard_map/ppermute | solution.py:26
  72.6 10.4 %copy-start.62 = (f32[3,8,8,32]{3,1,2,0:T(8,128)S(1)}, f32[3,8,8,32]{3,1,2,0:T(8,128)}, u32[]{:S(2)}) copy-start(f32[3,8,8,32]{3,1,2,0:T(8,128)} %slice.499) | copy-start | bytes 73732
  72.6 10.4 %copy-start.61 = (f32[3,8,8,32]{3,1,2,0:T(8,128)S(1)}, f32[3,8,8,32]{3,1,2,0:T(8,128)}, u32[]{:S(2)}) copy-start(f32[3,8,8,32]{3,1,2,0:T(8,128)} %slice.500) | copy-start | bytes 73732
  72.7 11.0 %copy-start.48 = (f32[1,8,16,256]{3,2,1,0:T(8,128)}, f32[1,8,16,256]{3,2,1,0:T(8,128)S(1)}, u32[]{:S(2)}) copy-start(f32[1,8,16,256]{3,2,1,0:T(8,128)S(1)} %copy.242) | copy-start | bytes 393220
  72.8 10.9 %copy-start.50 = (f32[1,8,16,256]{3,2,1,0:T(8,128)}, f32[1,8,16,256]{3,2,1,0:T(8,128)S(1)}, u32[]{:S(2)}) copy-start(f32[1,8,16,256]{3,2,1,0:T(8,128)S(1)} %copy.243) | copy-start | bytes 393220
  72.8 10.9 %copy-start.52 = (f32[1,8,16,256]{3,2,1,0:T(8,128)}, f32[1,8,16,256]{3,2,1,0:T(8,128)S(1)}, u32[]{:S(2)}) copy-start(f32[1,8,16,256]{3,2,1,0:T(8,128)S(1)} %copy.244) | copy-start | bytes 393220
  73.5 12.8 %copy-start.60 = (f32[3,8,8,32]{3,1,2,0:T(8,128)S(1)}, f32[3,8,8,32]{3,1,2,0:T(8,128)}, u32[]{:S(2)}) copy-start(f32[3,8,8,32]{3,1,2,0:T(8,128)} %slice.504) | copy-start | bytes 73732
  74.4 12.6 %copy-start.65 = (f32[4,8,1,258]{3,1,2,0:T(8,128)S(1)}, f32[4,8,1,258]{3,1,2,0:T(8,128)}, u32[]{:S(2)}) copy-start(f32[4,8,1,258]{3,1,2,0:T(8,128)} %copy-done.63) | copy-start | bytes 99076
  75.7 21.3 %collective-permute-start.4 = (f32[3,8,1,256]{3,1,2,0:T(8,128)}, f32[3,8,1,256]{3,1,2,0:T(8,128)}, u32[]{:S(2)}, u32[]{:S(2)}) collective-permute-start(f32[3,8,1,256]{3,1,2,0:T(8,128)} %copy.245), channel_id=1, source_target_pairs={{0,1},{1,2},{2,3},{3,4},{4,5},{5,6},{6,7},{8,9},{9,10},{10,11},{11... | collective-permute-start | bytes 73736 | tf_op jit(solution)/shard_map/ppermute | solution.py:24
  81.2 15.8 %collective-permute-start.5 = (f32[3,8,1,256]{3,1,2,0:T(8,128)}, f32[3,8,1,256]{3,1,2,0:T(8,128)}, u32[]{:S(2)}, u32[]{:S(2)}) collective-permute-start(f32[3,8,1,256]{3,1,2,0:T(8,128)} %copy.246), channel_id=1, source_target_pairs={{1,0},{2,1},{3,2},{4,3},{5,4},{6,5},{7,6},{9,8},{10,9},{11,10},{12... | collective-permute-start | bytes 73736 | tf_op jit(solution)/shard_map/ppermute | solution.py:26
  122.8 12.5 %all-to-all-start = ((f32[8,4,768]{2,1,0:T(4,128)}), f32[8,4,768]{2,1,0:T(4,128)S(1)}, u32[]{:S(2)}, u32[]{:S(2)}) async-start(f32[8,4,768]{2,1,0:T(4,128)} %reshape.321), calls=%async_computation | async-start | bytes 196608 | tf_op jit(solution)/shard_map/all_to_all | solution.py:203
  135.3 66.5 %all-to-all-start.1 = ((f32[8,4,768]{2,1,0:T(4,128)}), f32[8,4,768]{2,1,0:T(4,128)}, u32[]{:S(2)}, u32[]{:S(2)}) async-start(f32[8,4,768]{2,1,0:T(4,128)} %reshape.327), calls=%async_computation.1 | async-start | bytes 196608 | tf_op jit(solution)/shard_map/all_to_all | solution.py:203
  192.3 153.8 %copy-start.10 = (f32[1,4,32,1024]{3,2,1,0:T(8,128)}, f32[1,4,32,1024]{3,2,1,0:T(8,128)S(1)}, u32[]{:S(2)}) copy-start(f32[1,4,32,1024]{3,2,1,0:T(8,128)S(1)} %get-tuple-element.59) | copy-start | bytes 1572868
  201.9 82.0 %all-to-all-start.2 = ((f32[8,4,768]{2,1,0:T(4,128)}), f32[8,4,768]{2,1,0:T(4,128)}, u32[]{:S(2)}, u32[]{:S(2)}) async-start(f32[8,4,768]{2,1,0:T(4,128)} %reshape.333), calls=%async_computation.2 | async-start | bytes 196608 | tf_op jit(solution)/shard_map/all_to_all | solution.py:203
  283.9 84.5 %all-to-all-start.3 = ((f32[8,4,768]{2,1,0:T(4,128)}), f32[8,4,768]{2,1,0:T(4,128)}, u32[]{:S(2)}, u32[]{:S(2)}) async-start(f32[8,4,768]{2,1,0:T(4,128)} %reshape.339), calls=%async_computation.3 | async-start | bytes 196608 | tf_op jit(solution)/shard_map/all_to_all | solution.py:203
  346.1 10.5 %copy-start.29 = (f32[4,32,1024]{2,1,0:T(8,128)S(1)}, f32[4,32,1024]{2,1,0:T(8,128)}, u32[]{:S(2)}) copy-start(f32[4,32,1024]{2,1,0:T(8,128)} %get-tuple-element.15) | copy-start | bytes 1572868
  346.1 10.5 %copy-start.31 = (f32[1,4,32,1024]{3,2,1,0:T(8,128)S(1)}, f32[1,4,32,1024]{3,2,1,0:T(8,128)}, u32[]{:S(2)}) copy-start(f32[1,4,32,1024]{3,2,1,0:T(8,128)} %copy-done.30) | copy-start | bytes 1572868
  346.1 10.5 %copy-start.33 = (f32[1,4,32,1024]{3,2,1,0:T(8,128)S(1)}, f32[1,4,32,1024]{3,2,1,0:T(8,128)}, u32[]{:S(2)}) copy-start(f32[1,4,32,1024]{3,2,1,0:T(8,128)} %copy-done.32) | copy-start | bytes 1572868
  346.1 10.5 %copy-start.35 = (f32[1,4,32,1024]{3,2,1,0:T(8,128)S(1)}, f32[1,4,32,1024]{3,2,1,0:T(8,128)}, u32[]{:S(2)}) copy-start(f32[1,4,32,1024]{3,2,1,0:T(8,128)} %copy-done.34) | copy-start | bytes 1572868
  346.1 10.5 %copy-start.42 = (f32[1,4,32,1024]{3,2,1,0:T(8,128)S(1)}, f32[1,4,32,1024]{3,2,1,0:T(8,128)}, u32[]{:S(2)}) copy-start(f32[1,4,32,1024]{3,2,1,0:T(8,128)} %get-tuple-element.12) | copy-start | bytes 1572868
  346.1 10.5 %copy-start.43 = (f32[4,32,1024]{2,1,0:T(8,128)S(1)}, f32[4,32,1024]{2,1,0:T(8,128)}, u32[]{:S(2)}) copy-start(f32[4,32,1024]{2,1,0:T(8,128)} %get-tuple-element.13) | copy-start | bytes 1572868
  416.9 53.4 %copy-start.36 = (f32[4,3,32,1024]{3,2,1,0:T(8,128)}, f32[4,3,32,1024]{3,2,1,0:T(8,128)S(1)}, u32[]{:S(2)}) copy-start(f32[4,3,32,1024]{3,2,1,0:T(8,128)S(1)} %bitcast_add_fusion) | copy-start | bytes 4718596
  488.1 31.5 %copy-start.84 = (s32[64]{0:T(128)S(1)}, s32[64]{0:T(128)}, u32[]{:S(2)}) copy-start(s32[64]{0:T(128)} %sub.185) | copy-start | bytes 772
  (63 other events, 224.3 us)
where the time goes:
time: 543 us; the launch traced here: 532 us
  local copies, waits for them, and re-layouts  364 us (67%)
  other arithmetic  86.7 us (16%)
  starting transfers between devices  40.5 us (7%)
  blocking collectives  31.2 us (6%)
  matrix products  5.64 us (1%)
    reshape x1, local copies, waits for them, and re-layouts, restrict(): shaped = fields.reshape(3, NZC, RATIO, BLK, RATIO, BLK, RATIO)  53.4 us
    another operation x12, local copies, waits for them, and re-layouts, patch_step(): jnp.tile(ghosts[0], (1, 1, edge_len))  41.4 us
    another operation x12, local copies, waits for them, and re-layouts, patch_step(): jnp.tile(ghosts[1], (1, 1, edge_len))  41 us
    add x5, other arithmetic, combine(): summed = summed + harmonic(conduct, coeffs) * (values - center)  35.8 us
    all_gather x1, blocking collectives, per_device(): portion = lax.all_gather(averages, 'af', axis=0, tiled=True)  31.2 us
    reshape x4, local copies, waits for them, and re-layouts, patch_step(): jnp.repeat(ghosts[3], edge_len, axis=-1)  23.6 us
    all_to_all x4, starting transfers between devices, per_device(): lax.all_to_all(send_rows.reshape(af_count, slot_count, current.shape[1]),...  23.6 us
    reshape x4, local copies, waits for them, and re-layouts, patch_step(): jnp.repeat(ghosts[2], edge_len, axis=-1)  23.6 us
  transfers between devices with their start and end apart: 10, of which 2 were waited for; matrix products, arithmetic and copies ran while one was open for 50% of the time, Pallas kernels for 0%

commit v1 on v0

v1 whole, which is shorter than its diff:
```python
import functools

import jax
import jax.numpy as jnp
import ml_dtypes
import numpy as np
from jax import lax
from jax.experimental import pallas as pl
from jax.experimental.pallas import tpu as pltpu
from jax.sharding import PartitionSpec as P

NZC = 8
RATIO = 4
BLK = 8
SPECIES = 3
EDGE = BLK * RATIO
FZ = NZC * RATIO
LANES = 128
TILES = EDGE * EDGE // LANES
STRIDE = 48
PAD = 8
FACES = 4
STRIP_ROWS = 2 * SPECIES * NZC
AVG_ROWS = SPECIES * NZC * BLK

DT_COARSE = 1.0 / 28.0
DIFFUSE = (1.0, 0.7, 0.45)
SIGNS = (-1.0, -1.0, 1.0)
FINE_SCALE = RATIO * RATIO * DT_COARSE / RATIO
DT_FINE = DT_COARSE / RATIO


def lane_ids(shape):
    return lax.broadcasted_iota(jnp.int32, shape, len(shape) - 1)


def roll_lanes(values, shift):
    width = values.shape[-1]
    shift = shift % width
    return values if shift == 0 else pltpu.roll(values, shift, values.ndim - 1)


def split_pair(values):
    high = values.astype(jnp.bfloat16)
    low = (values - high.astype(jnp.float32)).astype(jnp.bfloat16)
    return high, low


def harmonic(first, second):
    summed = first + second
    positive = summed > 0.0
    return jnp.where(positive, 2.0 * first * second / jnp.where(positive, summed, 1.0), 0.0)


def block_vectors(boxes_ref, group, block_cols, block_rows):
    lanes = group * BLK
    patch = lane_ids((8, lanes)) // BLK
    base = lax.axis_index("col") * group
    first_col = lax.axis_index("af") * block_cols
    first_row = lax.axis_index("col") * block_rows
    columns = jnp.full((8, lanes), -9, jnp.int32)
    starts = jnp.full((8, lanes), -9, jnp.int32)
    for q in range(group):
        here = patch == q
        columns = jnp.where(here, boxes_ref[base + q, 0] - first_col, columns)
        starts = jnp.where(here, (boxes_ref[base + q, 1] - first_row) * BLK, starts)
    return columns, starts + lane_ids((8, lanes)) % BLK


def selector(columns, cells, column, cells_y):
    wanted = jnp.where(columns == column, cells, -1)
    lanes = wanted.shape[-1]
    row = lax.broadcasted_iota(jnp.int32, (8, lanes), 0)
    pieces = [
        jnp.where(row + 8 * piece == wanted, 1.0, 0.0).astype(jnp.float32)
        for piece in range(cells_y // 8)
    ]
    return jnp.concatenate(pieces, axis=0).astype(jnp.bfloat16)


def edges_kernel(state_ref, kappa_ref, xlo_ref, xhi_ref, ylo_ref, yhi_ref, *, cells_x, cells_y):
    planes = SPECIES * NZC
    lane = lane_ids((cells_x, LANES))
    low = jnp.zeros((cells_x, LANES), jnp.float32)
    high = jnp.zeros((cells_x, LANES), jnp.float32)
    for plane in range(planes + NZC):
        if plane < planes:
            ref, start = state_ref, plane * cells_x
        else:
            ref, start = kappa_ref, (plane - planes) * cells_x
        first = ref[start : start + cells_x, 0:LANES]
        last = ref[start : start + cells_x, cells_y - LANES : cells_y]
        xlo_ref[plane : plane + 1, :] = ref[start : start + 1, :]
        xhi_ref[plane : plane + 1, :] = ref[start + cells_x - 1 : start + cells_x, :]
        low = jnp.where(lane == plane, roll_lanes(first, plane), low)
        high = jnp.where(lane == plane, roll_lanes(last, plane + 1), high)
    ylo_ref[...] = low
    yhi_ref[...] = high


def coarse_kernel(
    boxes_ref,
    state_ref,
    kappa_ref,
    rate_ref,
    xl_ref,
    xr_ref,
    yl_ref,
    yr_ref,
    new_ref,
    send_ref,
    padded,
    fresh,
    *,
    cells_x,
    cells_y,
    group,
    slots,
):
    halves = cells_y // LANES
    span = cells_x + 2 * PAD

    def base(field, half, z):
        return ((field * halves + half) * NZC + z) * span

    for field in range(SPECIES + 1):
        for half in range(halves):
            cols = pl.ds(half * LANES, LANES)
            for z in range(NZC):
                if field < SPECIES:
                    start = (field * NZC + z) * cells_x
                    plane = state_ref[start : start + cells_x, cols]
                else:
                    plane = kappa_ref[z * cells_x : (z + 1) * cells_x, cols]
                at = base(field, half, z) + PAD
                padded[at : at + cells_x, :] = plane
            at = base(field, half, 0) + PAD
            rows = slice(field * NZC, (field + 1) * NZC)
            padded[pl.ds(at - 1, NZC, stride=span), :] = xl_ref[rows, cols]
            padded[pl.ds(at + cells_x, NZC, stride=span), :] = xr_ref[rows, cols]

    lane = lane_ids((cells_x, LANES))
    lower_edge = yl_ref[...]
    upper_edge = yr_ref[...]

    def load(field, half, z, shift):
        at = base(field, half, z) + PAD + shift
        return padded[at : at + cells_x, :]

    def along_y(field, half, z):
        plane = field * NZC + z
        here = load(field, half, z, 0)
        if half + 1 < halves:
            after = roll_lanes(load(field, half + 1, z, 0), -1)
        else:
            after = roll_lanes(upper_edge, LANES - 1 - plane)
        if half > 0:
            before = roll_lanes(load(field, half - 1, z, 0), 1)
        else:
            before = roll_lanes(lower_edge, -plane)
        return (
            jnp.where(lane == LANES - 1, after, roll_lanes(here, -1)),
            jnp.where(lane == 0, before, roll_lanes(here, 1)),
        )

    def neighbours(field, half, z):
        found = [load(field, half, z, 1), load(field, half, z, -1), *along_y(field, half, z)]
        if z + 1 < NZC:
            found.append(load(field, half, z + 1, 0))
        if z > 0:
            found.append(load(field, half, z - 1, 0))
        return found

    for z in range(NZC):
        for half in range(halves):
            cols = pl.ds(half * LANES, LANES)
            conduct = load(SPECIES, half, z, 0)
            coeffs = [harmonic(conduct, other) for other in neighbours(SPECIES, half, z)]
            centers = [load(field, half, z, 0) for field in range(SPECIES)]
            forward = (DT_COARSE * rate_ref[z * cells_x : (z + 1) * cells_x, cols]) * (
                centers[0] * centers[1] - centers[2]
            )
            for field in range(SPECIES):
                center = centers[field]
                flux = jnp.zeros_like(center)
                for coeff, other in zip(coeffs, neighbours(field, half, z)):
                    flux = flux + coeff * (other - center)
                start = (field * NZC + z) * cells_x
                result = center + (DT_COARSE * DIFFUSE[field]) * flux + SIGNS[field] * forward
                new_ref[start : start + cells_x, cols] = result
                start = ((field * halves + half) * NZC + z) * cells_x
                fresh[start : start + cells_x, :] = result

    def rows_at(row):
        columns = []
        for half in range(halves):
            pieces = []
            for field in range(SPECIES):
                pieces.append(padded[pl.ds(base(field, half, 0) + PAD + row, NZC, stride=span), :])
            for field in range(SPECIES):
                start = (field * halves + half) * NZC * cells_x
                pieces.append(fresh[pl.ds(start + row, NZC, stride=cells_x), :])
            columns.append(jnp.concatenate(pieces, axis=0))
        return jnp.concatenate(columns, axis=1)

    block_cols = cells_x // BLK
    spot = lane_ids((STRIP_ROWS, cells_y)) % BLK
    lower_y = []
    upper_y = []
    for column in range(block_cols):
        below = jnp.zeros((STRIP_ROWS, cells_y), jnp.float32)
        above = jnp.zeros((STRIP_ROWS, cells_y), jnp.float32)
        for x in range(BLK):
            strip = rows_at(column * BLK + x)
            below = jnp.where(spot == x, roll_lanes(strip, x + 1), below)
            above = jnp.where(spot == x, roll_lanes(strip, x - BLK), above)
        lower_y.append(below)
        upper_y.append(above)

    columns, cells = block_vectors(boxes_ref, group, block_cols, cells_y // BLK)
    faces = [None] * FACES

    def add(face, part):
        faces[face] = part if faces[face] is None else faces[face] + part

    for column in range(-1, block_cols + 1):
        members = []
        if column >= 1:
            members.append((0, rows_at(column * BLK - 1)))
        if column < block_cols - 1:
            members.append((1, rows_at(column * BLK + BLK)))
        if 0 <= column < block_cols:
            members.append((2, lower_y[column]))
            members.append((3, upper_y[column]))
        operands = []
        for _, rows in members:
            operands.extend(split_pair(rows))
        moved = jnp.dot(
            jnp.concatenate(operands, axis=0),
            selector(columns, cells, column, cells_y),
            preferred_element_type=jnp.float32,
        )
        for index, (face, _) in enumerate(members):
            at = 2 * index * STRIP_ROWS
            add(face, moved[at : at + STRIP_ROWS] + moved[at + STRIP_ROWS : at + 2 * STRIP_ROWS])

    width = slots * BLK
    part = lane_ids((STRIP_ROWS, LANES)) // width
    for target in range(group // slots):
        first = target * width
        tile = first // LANES * LANES
        chunk = jnp.zeros((STRIP_ROWS, LANES), jnp.float32)
        for face in range(FACES):
            piece = faces[face][:, tile : tile + LANES]
            chunk = jnp.where(part == face, roll_lanes(piece, face * width - (first - tile)), chunk)
        send_ref[target] = chunk


def ghost_table():
    table = np.zeros((LANES, EDGE * EDGE), np.float32)
    x, y = np.divmod(np.arange(EDGE * EDGE), EDGE)
    width = LANES // FACES
    for pos in range(BLK):
        table[0 * width + pos] = (x == 0) & (y // RATIO == pos)
        table[1 * width + pos] = (x == EDGE - 1) & (y // RATIO == pos)
        table[2 * width + pos] = (y == 0) & (x // RATIO == pos)
        table[3 * width + pos] = (y == EDGE - 1) & (x // RATIO == pos)
    return np.concatenate([table, table]).astype(ml_dtypes.bfloat16)


def plane_table():
    rows = np.arange(2 * SPECIES * FZ)
    return (rows[:, None] // RATIO == np.arange(STRIP_ROWS)[None, :]).astype(ml_dtypes.bfloat16)


def mean_table():
    lane = np.arange(LANES)
    table = (lane[:, None] % EDGE // RATIO == lane[None, :] % BLK) / float(RATIO**3)
    return np.concatenate([table, table]).astype(ml_dtypes.bfloat16)


def fine_kernel(
    state_ref,
    kappa_ref,
    rate_ref,
    strips_ref,
    ghost_ref,
    plane_ref,
    mean_ref,
    out_ref,
    avg_ref,
    first,
    second,
    conduct,
    upward,
    coeffs,
    still,
    drift,
    *,
    slots,
):
    slot = pl.program_id(0)
    sources = strips_ref.shape[0]
    ztiles = FZ // 8

    def at(block, tile):
        return block * STRIDE + PAD + 8 * tile

    @pl.when(slot == 0)
    def _():
        edge = jnp.zeros((PAD, LANES), jnp.float32)
        for ref in (first, second, conduct, upward):
            for block in range(ref.shape[0] // STRIDE):
                ref[block * STRIDE : block * STRIDE + PAD, :] = edge
                ref[block * STRIDE + PAD + FZ : (block + 1) * STRIDE, :] = edge

    for tile in range(TILES):
        cols = pl.ds(tile * LANES, LANES)
        for field in range(SPECIES):
            row = at(field * TILES + tile, 0)
            first[row : row + FZ, :] = state_ref[0, field, :, cols]
        row = at(tile, 0)
        conduct[row : row + FZ, :] = kappa_ref[0, :, cols]

    gathered = strips_ref[0]
    for source in range(1, sources):
        gathered = gathered + strips_ref[source]
    gathered = pltpu.roll(gathered, (LANES - slot * BLK) % LANES, 1)
    half = STRIP_ROWS // 2
    gathered = jnp.concatenate(
        [gathered[:half], (gathered[half:] - gathered[:half]) * (1.0 / RATIO)], axis=0
    )
    stretched = jnp.dot(
        plane_ref[...],
        jnp.concatenate(split_pair(gathered), axis=1),
        preferred_element_type=jnp.float32,
    ).astype(jnp.bfloat16)
    for tile in range(TILES):
        ghosts = jnp.dot(
            stretched,
            ghost_ref[:, tile * LANES : (tile + 1) * LANES],
            preferred_element_type=jnp.float32,
        )
        scale = conduct[pl.ds(at(tile, 0), FZ), :] * FINE_SCALE
        for field in range(SPECIES):
            row = (field * TILES + tile) * FZ
            still[row : row + FZ, :] = scale * ghosts[field * FZ : (field + 1) * FZ]
            drift[row : row + FZ, :] = (
                scale * ghosts[(SPECIES + field) * FZ : (SPECIES + field + 1) * FZ]
            )

    lane = lane_ids((8, LANES))
    column = lane % EDGE
    side_y = jnp.where((column == 0) | (column == EDGE - 1), 1.0, 0.0)

    def face(one, other):
        return (2.0 * FINE_SCALE) * one * other / (one + other)

    def keep(kind, tile, ztile, values):
        row = ((kind * TILES + tile) * ztiles) * 8
        coeffs[pl.ds(pl.multiple_of(row + 8 * ztile, 8), 8), :] = values

    def prepare(ztile, carry):
        def here(tile, shift):
            return conduct[pl.ds(tile * STRIDE + PAD + shift + 8 * ztile, 8), :]

        centers = [here(tile, 0) for tile in range(TILES)]
        turned = [roll_lanes(center, -EDGE) for center in centers]
        next_x = []
        for tile in range(TILES):
            other = jnp.where(lane < LANES - EDGE, turned[tile], turned[(tile + 1) % TILES])
            values = face(centers[tile], other)
            if tile == TILES - 1:
                values = jnp.where(lane < LANES - EDGE, values, 0.0)
            next_x.append(values)
        back = [roll_lanes(values, EDGE) for values in next_x]
        for tile in range(TILES):
            center = centers[tile]
            prev_x = jnp.where(lane >= EDGE, back[tile], back[tile - 1])
            next_y = jnp.where(column < EDGE - 1, face(center, roll_lanes(center, -1)), 0.0)
            prev_y = roll_lanes(next_y, 1)
            next_z = face(center, here(tile, 1))
            prev_z = face(center, here(tile, -1))
            sides = side_y
            if tile == 0:
                sides = sides + jnp.where(lane < EDGE, 1.0, 0.0)
            if tile == TILES - 1:
                sides = sides + jnp.where(lane >= LANES - EDGE, 1.0, 0.0)
            total = (next_x[tile] + prev_x) + (next_y + prev_y) + (next_z + prev_z)
            total = total + (FINE_SCALE * sides) * center
            upward[pl.ds(tile * STRIDE + PAD + 8 * ztile, 8), :] = next_z
            keep(0, tile, ztile, next_x[tile])
            keep(1, tile, ztile, prev_x)
            keep(2, tile, ztile, next_y)
            keep(3, tile, ztile, prev_y)
            keep(4, tile, ztile, total)
            keep(
                5,
                tile,
                ztile,
                DT_FINE
                * rate_ref[0, pl.ds(pl.multiple_of(8 * ztile, 8), 8), pl.ds(tile * LANES, LANES)],
            )
        return carry

    lax.fori_loop(0, ztiles, prepare, 0)

    def substep(source, target, step, ztile):
        def value(field, tile, shift):
            return source[pl.ds((field * TILES + tile) * STRIDE + PAD + shift + 8 * ztile, 8), :]

        def get(kind, tile):
            row = ((kind * TILES + tile) * ztiles) * 8
            return coeffs[pl.ds(pl.multiple_of(row + 8 * ztile, 8), 8), :]

        centers = [[value(field, tile, 0) for tile in range(TILES)] for field in range(SPECIES)]
        down = [[roll_lanes(values, -EDGE) for values in row] for row in centers]
        up = [[roll_lanes(values, EDGE) for values in row] for row in centers]
        for tile in range(TILES):
            next_x, prev_x, next_y, prev_y, total, rate = [get(kind, tile) for kind in range(6)]
            next_z = upward[pl.ds(tile * STRIDE + PAD + 8 * ztile, 8), :]
            prev_z = upward[pl.ds(tile * STRIDE + PAD - 1 + 8 * ztile, 8), :]
            forward = rate * (
                centers[0][tile] * centers[1][tile] - centers[2][tile]
            )
            for field in range(SPECIES):
                center = centers[field][tile]
                ahead = jnp.where(
                    lane < LANES - EDGE, down[field][tile], down[field][(tile + 1) % TILES]
                )
                behind = jnp.where(lane >= EDGE, up[field][tile], up[field][tile - 1])
                row = (field * TILES + tile) * FZ
                spot = pl.ds(pl.multiple_of(row + 8 * ztile, 8), 8)
                flux = (next_x * ahead + prev_x * behind) + (
                    next_y * roll_lanes(center, -1) + prev_y * roll_lanes(center, 1)
                )
                flux = flux + (
                    next_z * value(field, tile, 1) + prev_z * value(field, tile, -1)
                )
                flux = flux + (still[spot, :] + step * drift[spot, :]) - total * center
                result = center + DIFFUSE[field] * flux + SIGNS[field] * forward
                target[
                    pl.ds(
                        pl.multiple_of((field * TILES + tile) * STRIDE + PAD + 8 * ztile, 8), 8
                    ),
                    :,
                ] = result

    def pair(index, carry):
        def go(source, target, step):
            def body(ztile, inner):
                substep(source, target, step, ztile)
                return inner

            lax.fori_loop(0, ztiles, body, 0)

        start = (2 * index).astype(jnp.float32)
        go(first, second, start)
        go(second, first, start + 1.0)
        return carry

    lax.fori_loop(0, RATIO // 2, pair, 0)

    for tile in range(TILES):
        for field in range(SPECIES):
            row = at(field * TILES + tile, 0)
            out_ref[0, field, :, pl.ds(tile * LANES, LANES)] = first[row : row + FZ, :]

    sums = []
    for field in range(SPECIES):
        for plane in range(NZC):
            start = field * TILES * STRIDE + PAD + RATIO * plane
            part = first[pl.ds(start, TILES, stride=STRIDE), :]
            for z in range(1, RATIO):
                part = part + first[pl.ds(start + z, TILES, stride=STRIDE), :]
            sums.append(part)
    means = jnp.dot(
        jnp.concatenate(split_pair(jnp.concatenate(sums, axis=0)), axis=1),
        mean_ref[...],
        preferred_element_type=jnp.float32,
    )
    quarter = AVG_ROWS // FACES
    spot = lane_ids((quarter, LANES)) // BLK
    chunk = avg_ref[0]
    for part in range(FACES):
        chunk = jnp.where(
            spot == part * slots + slot, means[part * quarter : (part + 1) * quarter], chunk
        )
    avg_ref[0] = chunk

    @pl.when(slot == slots - 1)
    def _():
        for target in range(1, avg_ref.shape[0]):
            avg_ref[target] = chunk


def place_kernel(boxes_ref, avg_ref, new_ref, out_ref, *, cells_x, cells_y, group, slots):
    width = slots * BLK
    quarter = AVG_ROWS // FACES
    per_tile = LANES // width
    part = lane_ids((quarter, LANES)) // width
    columns = []
    for tile in range(group * BLK // LANES):
        rows = []
        for index in range(FACES):
            merged = jnp.zeros((quarter, LANES), jnp.float32)
            for place in range(per_tile):
                piece = roll_lanes(avg_ref[tile * per_tile + place], (place - index) * width)
                merged = jnp.where(part == place, piece, merged)
            rows.append(merged)
        columns.append(jnp.concatenate(rows, axis=0))
    averages = jnp.concatenate(columns, axis=1)
    high, low = split_pair(averages)
    ones = jnp.ones((16, averages.shape[1]), jnp.bfloat16)
    stacked = jnp.concatenate([high, low, ones], axis=0)

    block_cols = cells_x // BLK
    block_of, cells = block_vectors(boxes_ref, group, block_cols, cells_y // BLK)
    for column in range(block_cols):
        placed = lax.dot_general(
            stacked,
            selector(block_of, cells, column, cells_y),
            (((1,), (1,)), ((), ())),
            preferred_element_type=jnp.float32,
        )
        covered = placed[2 * AVG_ROWS : 2 * AVG_ROWS + 8] > 0.5
        for plane in range(SPECIES * NZC):
            values = (
                placed[plane * BLK : (plane + 1) * BLK]
                + placed[AVG_ROWS + plane * BLK : AVG_ROWS + (plane + 1) * BLK]
            )
            row = plane * cells_x + column * BLK
            out_ref[row : row + BLK, :] = jnp.where(covered, values, new_ref[row : row + BLK, :])


def vmem():
    return pl.BlockSpec(memory_space=pltpu.VMEM)


def smem():
    return pl.BlockSpec(memory_space=pltpu.SMEM)


def f32(*shape):
    return jax.ShapeDtypeStruct(shape, jnp.float32)


PARAMS = pltpu.CompilerParams(vmem_limit_bytes=40 * 1024 * 1024)


def shifted(values, axis, step):
    count = lax.axis_size(axis)
    pairs = [(i, i + step) for i in range(count) if 0 <= i + step < count]
    return lax.ppermute(values, axis, pairs)


def exchange(chunks):
    return lax.all_to_all(chunks, "af", split_axis=0, concat_axis=0, tiled=True)


def per_device(
    coarse_state, coarse_kappa, coarse_rate, fine_state, fine_kappa, fine_rate, boxes, cover
):
    af_count = lax.axis_size("af")
    slots = fine_state.shape[0]
    cells_x, cells_y = coarse_state.shape[2:]
    group = af_count * slots
    planes = SPECIES * NZC
    state = coarse_state.reshape(planes * cells_x, cells_y)
    kappa = coarse_kappa.reshape(NZC * cells_x, cells_y)
    rate = coarse_rate.reshape(NZC * cells_x, cells_y)
    sizes = dict(cells_x=cells_x, cells_y=cells_y)

    xlo, xhi, ylo, yhi = pl.pallas_call(
        functools.partial(edges_kernel, **sizes),
        out_shape=[f32(planes + NZC, cells_y)] * 2 + [f32(cells_x, LANES)] * 2,
        in_specs=[vmem()] * 2,
        out_specs=[vmem()] * 4,
        compiler_params=PARAMS,
        name="edges",
    )(state, kappa)
    xl = shifted(xhi, "af", 1)
    xr = shifted(xlo, "af", -1)
    yl = shifted(yhi, "col", 1)
    yr = shifted(ylo, "col", -1)

    span = cells_x + 2 * PAD
    new, send = pl.pallas_call(
        functools.partial(coarse_kernel, group=group, slots=slots, **sizes),
        out_shape=[f32(planes * cells_x, cells_y), f32(af_count, STRIP_ROWS, LANES)],
        in_specs=[smem()] + [vmem()] * 7,
        out_specs=[vmem()] * 2,
        scratch_shapes=[
            pltpu.VMEM(((SPECIES + 1) * (cells_y // LANES) * NZC * span, LANES), jnp.float32),
            pltpu.VMEM((planes * cells_x * (cells_y // LANES), LANES), jnp.float32),
        ],
        compiler_params=PARAMS,
        name="coarse",
    )(boxes, state, kappa, rate, xl, xr, yl, yr)

    strips = exchange(send)

    blocks = SPECIES * TILES
    fine_out, averages = pl.pallas_call(
        functools.partial(fine_kernel, slots=slots),
        grid=(slots,),
        out_shape=[f32(*fine_state.shape), f32(af_count, AVG_ROWS // FACES, LANES)],
        in_specs=[
            pl.BlockSpec((1, SPECIES, FZ, EDGE * EDGE), lambda s: (s, 0, 0, 0)),
            pl.BlockSpec((1, FZ, EDGE * EDGE), lambda s: (s, 0, 0)),
            pl.BlockSpec((1, FZ, EDGE * EDGE), lambda s: (s, 0, 0)),
        ]
        + [vmem()] * 4,
        out_specs=[
            pl.BlockSpec((1, SPECIES, FZ, EDGE * EDGE), lambda s: (s, 0, 0, 0)),
            pl.BlockSpec((af_count, AVG_ROWS // FACES, LANES), lambda s: (0, 0, 0)),
        ],
        scratch_shapes=[
            pltpu.VMEM((blocks * STRIDE, LANES), jnp.float32),
            pltpu.VMEM((blocks * STRIDE, LANES), jnp.float32),
            pltpu.VMEM((TILES * STRIDE, LANES), jnp.float32),
            pltpu.VMEM((TILES * STRIDE, LANES), jnp.float32),
            pltpu.VMEM((6 * TILES * FZ, LANES), jnp.float32),
            pltpu.VMEM((blocks * FZ, LANES), jnp.float32),
            pltpu.VMEM((blocks * FZ, LANES), jnp.float32),
        ],
        compiler_params=PARAMS,
        name="fine",
    )(
        fine_state,
        fine_kappa,
        fine_rate,
        strips,
        jnp.asarray(ghost_table()),
        jnp.asarray(plane_table()),
        jnp.asarray(mean_table()),
    )

    arrived = exchange(averages)

    placed = pl.pallas_call(
        functools.partial(place_kernel, group=group, slots=slots, **sizes),
        out_shape=f32(planes * cells_x, cells_y),
        in_specs=[smem()] + [vmem()] * 2,
        out_specs=vmem(),
        compiler_params=PARAMS,
        name="place",
    )(boxes, arrived, new)
    return (placed.reshape(coarse_state.shape), fine_out)


def solution(mesh):
    return jax.shard_map(
        per_device,
        mesh=mesh,
        in_specs=(
            P(None, None, "af", "col"),
            P(None, "af", "col"),
            P(None, "af", "col"),
            P(("col", "af"), None, None, None),
            P(("col", "af"), None, None),
            P(("col", "af"), None, None),
            P(),
            P(),
        ),
        out_specs=(P(None, None, "af", "col"), P(("col", "af"), None, None, None)),
        check_vma=False,
    )
```

time: 543 us -> 74.7 us (0.14)
  the two profiles are of different devices: /device:TPU:2 before, /device:TPU:0 now
where the time goes in v1:
time: 74.7 us; the launch traced here: 74.1 us
  blocking collectives  27 us (36%)
  Pallas kernels  25.2 us (34%)
  local copies, waits for them, and re-layouts  9.78 us (13%)
  starting transfers between devices  8.92 us (12%)
  waiting for transfers between devices  2.54 us (3%)
    all_to_all x2, blocking collectives, exchange(): return lax.all_to_all(chunks, 'af', split_axis=0, concat_axis=0, tiled=True)  27 us
    pallas_call x1, Pallas kernels, per_device(): pl.pallas_call(functools.partial(fine_kernel, slots=slots), grid=(slots,)...  19 us
    unnamed x23, local copies, waits for them, and re-layouts  9.78 us
    ppermute x4, starting transfers between devices, shifted(): return lax.ppermute(values, axis, pairs)  8.92 us
    pallas_call x1, Pallas kernels, per_device(): pl.pallas_call(functools.partial(coarse_kernel, group=group, slots=slots,...  3.2 us
    pallas_call x1, Pallas kernels, per_device(): pl.pallas_call(functools.partial(place_kernel, group=group, slots=slots,...  2.82 us
    ppermute x4, waiting for transfers between devices, shifted(): return lax.ppermute(values, axis, pairs)  2.54 us
  transfers between devices with their start and end apart: 4, of which 1 were waited for; matrix products, arithmetic and copies ran while one was open for 1% of the time, Pallas kernels for 0%

profile of v1, /device:TPU:0, one launch (start us, length us, event | category | flops | bytes accessed | tf_op | source)
XLA Modules:
  0.0 74.1 jit_solution(11390626756230501221)
XLA Ops:
  0.6 0.0 copy-start
  0.6 1.0 %copy-done = f32[3,8,16,256]{3,2,1,0:T(8,128)S(1)} copy-done((f32[3,8,16,256]{3,2,1,0:T(8,128)S(1)}, f32[3,8,16,256]{3,2,1,0:T(8,128)}, u32[]{:S(2)}) %copy-start) | copy-done | bytes 393240
  1.6 0.0 copy-start.3
  1.6 0.9 %copy-done.3 = f32[8,16,256]{2,1,0:T(8,128)S(1)} copy-done((f32[8,16,256]{2,1,0:T(8,128)S(1)}, f32[8,16,256]{2,1,0:T(8,128)}, u32[]{:S(2)}) %copy-start.3) | copy-done | bytes 131096
  2.5 0.0 copy-start.5
  2.5 0.0 copy-start.9
  2.5 0.2 edges.1
  2.7 4.9 %collective-permute-start = (f32[32,256]{1,0:T(8,128)S(1)}, f32[32,256]{1,0:T(8,128)S(1)}, u32[]{:S(2)}, u32[]{:S(2)}) collective-permute-start(f32[32,256]{1,0:T(8,128)S(1)} %get-tuple-element.10), channel_id=1, source_target_pairs={{0,1},{1,2},{2,3},{3,4},{4,5},{5,6},{6,7},{8,9},{9,10},{10,11},{11... | collective-permute-start | bytes 98312 | tf_op jit(solution)/shard_map/ppermute | solution.py:554
  7.6 1.3 %collective-permute-start.1 = (f32[32,256]{1,0:T(8,128)S(1)}, f32[32,256]{1,0:T(8,128)S(1)}, u32[]{:S(2)}, u32[]{:S(2)}) collective-permute-start(f32[32,256]{1,0:T(8,128)S(1)} %get-tuple-element.11), channel_id=1, source_target_pairs={{1,0},{2,1},{3,2},{4,3},{5,4},{6,5},{7,6},{9,8},{10,9},{11,10},{12... | collective-permute-start | bytes 98312 | tf_op jit(solution)/shard_map/ppermute | solution.py:554
  8.9 1.5 %collective-permute-start.2 = (f32[16,128]{1,0:T(8,128)S(1)}, f32[16,128]{1,0:T(8,128)S(1)}, u32[]{:S(2)}, u32[]{:S(2)}) collective-permute-start(f32[16,128]{1,0:T(8,128)S(1)} %get-tuple-element.12), channel_id=1, source_target_pairs={{0,8},{8,16},{16,24},{1,9},{9,17},{17,25},{2,10},{10,18},{18,26},{... | collective-permute-start | bytes 24584 | tf_op jit(solution)/shard_map/ppermute | solution.py:554
  10.4 1.3 %collective-permute-start.3 = (f32[16,128]{1,0:T(8,128)S(1)}, f32[16,128]{1,0:T(8,128)S(1)}, u32[]{:S(2)}, u32[]{:S(2)}) collective-permute-start(f32[16,128]{1,0:T(8,128)S(1)} %get-tuple-element.13), channel_id=1, source_target_pairs={{8,0},{16,8},{24,16},{9,1},{17,9},{25,17},{10,2},{18,10},{26,18},{... | collective-permute-start | bytes 24584 | tf_op jit(solution)/shard_map/ppermute | solution.py:554
  11.7 0.8 %copy.13.boxes_ref = s32[128,2]{1,0:T(8,128)S(1)} copy(s32[128,2]{0,1:T(2,128)} %param.17) | data formatting | bytes 2048 | tf_op args[6]
  12.5 0.0 collective-permute-done.2.yl_ref
  12.5 2.5 %collective-permute-done.3.yr_ref = f32[16,128]{1,0:T(8,128)S(1)} collective-permute-done((f32[16,128]{1,0:T(8,128)S(1)}, f32[16,128]{1,0:T(8,128)S(1)}, u32[]{:S(2)}, u32[]{:S(2)}) %collective-permute-start.3) | collective-permute-done | bytes 8224 | tf_op jit(solution)/shard_map/ppermute | solution.py:554
  15.0 0.0 collective-permute-done.xl_ref
  15.0 0.0 collective-permute-done.1.xr_ref
  15.0 0.0 copy-start.1
  15.0 1.0 %copy-done.1 = f32[3,8,16,256]{3,2,1,0:T(8,128)S(1)} copy-done((f32[3,8,16,256]{3,2,1,0:T(8,128)S(1)}, f32[3,8,16,256]{3,2,1,0:T(8,128)}, u32[]{:S(2)}) %copy-start.1) | copy-done | bytes 393240
  16.0 0.0 copy-start.4
  16.0 0.9 %copy-done.4 = f32[8,16,256]{2,1,0:T(8,128)S(1)} copy-done((f32[8,16,256]{2,1,0:T(8,128)S(1)}, f32[8,16,256]{2,1,0:T(8,128)}, u32[]{:S(2)}) %copy-start.4) | copy-done | bytes 131096
  16.9 0.9 %copy-done.8 = f32[8,16,256]{2,1,0:T(8,128)S(1)} copy-done((f32[8,16,256]{2,1,0:T(8,128)S(1)}, f32[8,16,256]{2,1,0:T(8,128)}, u32[]{:S(2)}) %copy-start.8) | copy-done | bytes 131096
  17.8 3.2 %coarse.1 = (f32[384,256]{1,0:T(8,128)S(1)}, f32[8,48,128]{2,1,0:T(8,128)S(1)}) custom-call(s32[128,2]{1,0:T(8,128)S(1)} %copy.13.boxes_ref, f32[384,256]{1,0:T(8,128)S(1)} %bitcast.5, f32[128,256]{1,0:T(8,128)S(1)} %bitcast.7, f32[128,256]{1,0:T(8,128)S(1)} %bitcast.8, f32[32,256]{1,0:T(8,128)S(1)} %collective-permute-done.xl_ref, ...), custom_call_target="tpu_custom_call" | custom-call | tf_op jit(solution)/shard_map/coarse/pallas_call | solution.py:588
  21.0 14.7 %all_to_all.10.strips_ref = f32[8,48,128]{2,1,0:T(8,128)S(1)} all-to-all(f32[8,48,128]{2,1,0:T(8,128)S(1)} %get-tuple-element.14), channel_id=1, replica_groups=mesh['col'=4,'af'=8] {'af'}, dimensions={0} | all-to-all | bytes 393216 | tf_op jit(solution)/shard_map/all_to_all | solution.py:558
  35.8 0.0 copy-done.5
  35.8 0.0 copy-done.9
  35.8 1.4 %copy-done.2 = f32[4,3,32,1024]{3,2,1,0:T(8,128)S(1)} copy-done((f32[4,3,32,1024]{3,2,1,0:T(8,128)S(1)}, f32[4,3,32,1024]{3,2,1,0:T(8,128)}, u32[]{:S(2)}) %copy-start.2) | copy-done | bytes 1572888
  37.2 1.0 %copy-done.6 = f32[4,32,1024]{2,1,0:T(8,128)S(1)} copy-done((f32[4,32,1024]{2,1,0:T(8,128)S(1)}, f32[4,32,1024]{2,1,0:T(8,128)}, u32[]{:S(2)}) %copy-start.6) | copy-done | bytes 524312
  38.2 1.0 %copy-done.7 = bf16[256,1024]{1,0:T(8,128)(2,1)S(1)} copy-done((bf16[256,1024]{1,0:T(8,128)(2,1)S(1)}, bf16[256,1024]{1,0:T(8,128)(2,1)}, u32[]{:S(2)}) %copy-start.7) | copy-done | bytes 524312
  39.3 0.8 %copy-done.10 = bf16[192,48]{1,0:T(8,128)(2,1)S(1)} copy-done((bf16[192,48]{1,0:T(8,128)(2,1)S(1)}, bf16[192,48]{1,0:T(8,128)(2,1)}, u32[]{:S(2)}) %copy-start.10) | copy-done | bytes 18456
  40.1 19.0 %fine.1 = (f32[4,3,32,1024]{3,2,1,0:T(8,128)}, f32[8,48,128]{2,1,0:T(8,128)S(1)}) custom-call(f32[4,3,32,1024]{3,2,1,0:T(8,128)S(1)} %copy-done.2, f32[4,32,1024]{2,1,0:T(8,128)S(1)} %copy-done.5, f32[4,32,1024]{2,1,0:T(8,128)S(1)} %copy-done.6, f32[8,48,128]{2,1,0:T(8,128)S(1)} %all_to_all.10.strips_ref, bf16[256,1024]{1,0:T(8,128)(2,1)S(1)} %copy-done.7, ...), custom_call_target="tpu_custom_call" | custom-call | tf_op jit(solution)/shard_map/fine/pallas_call | solution.py:604
  59.1 12.3 %all_to_all.11.avg_ref = f32[8,48,128]{2,1,0:T(8,128)S(1)} all-to-all(f32[8,48,128]{2,1,0:T(8,128)S(1)} %get-tuple-element.15), channel_id=1, replica_groups=mesh['col'=4,'af'=8] {'af'}, dimensions={0} | all-to-all | bytes 393216 | tf_op jit(solution)/shard_map/all_to_all | solution.py:558
  71.3 2.8 %place.1 = f32[384,256]{1,0:T(8,128)} custom-call(s32[128,2]{1,0:T(8,128)S(1)} %copy.13.boxes_ref, f32[8,48,128]{2,1,0:T(8,128)S(1)} %all_to_all.11.avg_ref, f32[384,256]{1,0:T(8,128)S(1)} %get-tuple-element.16.new_ref), custom_call_target="tpu_custom_call" | custom-call | tf_op jit(solution)/shard_map/place/pallas_call | solution.py:641
  (5 shorter events, 0.0 us)
Async XLA Ops:
  0.6 1.0 %copy-start = (f32[3,8,16,256]{3,2,1,0:T(8,128)S(1)}, f32[3,8,16,256]{3,2,1,0:T(8,128)}, u32[]{:S(2)}) copy-start(f32[3,8,16,256]{3,2,1,0:T(8,128)} %param.11) | copy-start | bytes 1179652
  1.6 0.9 %copy-start.3 = (f32[8,16,256]{2,1,0:T(8,128)S(1)}, f32[8,16,256]{2,1,0:T(8,128)}, u32[]{:S(2)}) copy-start(f32[8,16,256]{2,1,0:T(8,128)} %param.12) | copy-start | bytes 393220
  2.5 33.2 %copy-start.5 = (f32[4,32,1024]{2,1,0:T(8,128)S(1)}, f32[4,32,1024]{2,1,0:T(8,128)}, u32[]{:S(2)}) copy-start(f32[4,32,1024]{2,1,0:T(8,128)} %kappa_ref.1) | copy-start | bytes 1572868
  2.5 33.2 %copy-start.9 = (bf16[256,128]{1,0:T(8,128)(2,1)S(1)}, bf16[256,128]{1,0:T(8,128)(2,1)}, u32[]{:S(2)}) copy-start(bf16[256,128]{1,0:T(8,128)(2,1)} %constant.8.clone.mean_ref) | copy-start | bytes 196612
  2.7 12.3 %collective-permute-start = (f32[32,256]{1,0:T(8,128)S(1)}, f32[32,256]{1,0:T(8,128)S(1)}, u32[]{:S(2)}, u32[]{:S(2)}) collective-permute-start(f32[32,256]{1,0:T(8,128)S(1)} %get-tuple-element.10), channel_id=1, source_target_pairs={{0,1},{1,2},{2,3},{3,4},{4,5},{5,6},{6,7},{8,9},{9,10},{10,11},{11... | collective-permute-start | bytes 98312 | tf_op jit(solution)/shard_map/ppermute | solution.py:554
  7.6 7.4 %collective-permute-start.1 = (f32[32,256]{1,0:T(8,128)S(1)}, f32[32,256]{1,0:T(8,128)S(1)}, u32[]{:S(2)}, u32[]{:S(2)}) collective-permute-start(f32[32,256]{1,0:T(8,128)S(1)} %get-tuple-element.11), channel_id=1, source_target_pairs={{1,0},{2,1},{3,2},{4,3},{5,4},{6,5},{7,6},{9,8},{10,9},{11,10},{12... | collective-permute-start | bytes 98312 | tf_op jit(solution)/shard_map/ppermute | solution.py:554
  8.9 3.6 %collective-permute-start.2 = (f32[16,128]{1,0:T(8,128)S(1)}, f32[16,128]{1,0:T(8,128)S(1)}, u32[]{:S(2)}, u32[]{:S(2)}) collective-permute-start(f32[16,128]{1,0:T(8,128)S(1)} %get-tuple-element.12), channel_id=1, source_target_pairs={{0,8},{8,16},{16,24},{1,9},{9,17},{17,25},{2,10},{10,18},{18,26},{... | collective-permute-start | bytes 24584 | tf_op jit(solution)/shard_map/ppermute | solution.py:554
  10.4 4.6 %collective-permute-start.3 = (f32[16,128]{1,0:T(8,128)S(1)}, f32[16,128]{1,0:T(8,128)S(1)}, u32[]{:S(2)}, u32[]{:S(2)}) collective-permute-start(f32[16,128]{1,0:T(8,128)S(1)} %get-tuple-element.13), channel_id=1, source_target_pairs={{8,0},{16,8},{24,16},{9,1},{17,9},{25,17},{10,2},{18,10},{26,18},{... | collective-permute-start | bytes 24584 | tf_op jit(solution)/shard_map/ppermute | solution.py:554
  15.0 1.0 %copy-start.1 = (f32[3,8,16,256]{3,2,1,0:T(8,128)S(1)}, f32[3,8,16,256]{3,2,1,0:T(8,128)}, u32[]{:S(2)}) copy-start(f32[3,8,16,256]{3,2,1,0:T(8,128)} %param.11) | copy-start | bytes 1179652
  16.0 0.9 %copy-start.4 = (f32[8,16,256]{2,1,0:T(8,128)S(1)}, f32[8,16,256]{2,1,0:T(8,128)}, u32[]{:S(2)}) copy-start(f32[8,16,256]{2,1,0:T(8,128)} %param.12) | copy-start | bytes 393220
  16.9 0.9 %copy-start.8 = (f32[8,16,256]{2,1,0:T(8,128)S(1)}, f32[8,16,256]{2,1,0:T(8,128)}, u32[]{:S(2)}) copy-start(f32[8,16,256]{2,1,0:T(8,128)} %param.13) | copy-start | bytes 393220
  35.8 1.4 %copy-start.2 = (f32[4,3,32,1024]{3,2,1,0:T(8,128)S(1)}, f32[4,3,32,1024]{3,2,1,0:T(8,128)}, u32[]{:S(2)}) copy-start(f32[4,3,32,1024]{3,2,1,0:T(8,128)} %state_ref.1) | copy-start | bytes 4718596
  37.2 1.0 %copy-start.6 = (f32[4,32,1024]{2,1,0:T(8,128)S(1)}, f32[4,32,1024]{2,1,0:T(8,128)}, u32[]{:S(2)}) copy-start(f32[4,32,1024]{2,1,0:T(8,128)} %rate_ref.1) | copy-start | bytes 1572868
  38.2 1.0 %copy-start.7 = (bf16[256,1024]{1,0:T(8,128)(2,1)S(1)}, bf16[256,1024]{1,0:T(8,128)(2,1)}, u32[]{:S(2)}) copy-start(bf16[256,1024]{1,0:T(8,128)(2,1)} %constant.6.clone.ghost_ref) | copy-start | bytes 1572868
  39.3 0.8 %copy-start.10 = (bf16[192,48]{1,0:T(8,128)(2,1)S(1)}, bf16[192,48]{1,0:T(8,128)(2,1)}, u32[]{:S(2)}) copy-start(bf16[192,48]{1,0:T(8,128)(2,1)} %constant.7.clone.plane_ref) | copy-start | bytes 55300
